TPU v7x, 512 devices: a whole 4x4x16 slice. The times are simulated.
512 devices in a mesh: seq: 64 (over x, z), head: 8 (over y, core).
Axes of the slice: x: 4, y: 4, z: 16, core: 2. Of those that a mesh axis runs over, the one named last changes fastest.
Arguments:
- queries: bfloat16 [8192, 16, 128], P('seq', 'head'), may hold values from -21 to 21
- seq_keys: bfloat16 [8192, 16, 128], P('seq', 'head'), may hold values from -6 to 6
- seq_values: bfloat16 [8192, 16, 128], P('seq', 'head'), may hold values from -24 to 24
- memory_keys: bfloat16 [8192, 16, 128], P('seq', 'head'), may hold values from -6 to 6
- memory_values: bfloat16 [8192, 16, 128], P('seq', 'head'), may hold values from -24 to 24
- retrieval: int32 [64, 8], P('seq'), may hold values from 0 to 63, all different within a row
- fifo_head: int32 [1], replicated, may hold values from 0 to 63
- head_gate: float32 [16], P('head'), may hold values from -2 to 2
- norm_gain: float32 [16, 128], P('head'), may hold values from 0.1 to 1.9
Outputs:
- attended: bfloat16 [8192, 16, 128], P('seq', 'head')
Inputs may be any that keep to these rules, and one draw needn't show every extreme that they name: `retrieval`: each row names 8 different memory blocks.
All inputs are finite; a program needn't handle non-finite values.
Results may differ from a plain program's by a relative error of at most 0.029.
Values may be sent and summed in bfloat16 or wider, within the bound.
No kernel may reach another device: no remote copies, remote signals or barrier semaphores. Data moves between devices by JAX's collectives and lax.ppermute only.
A program may use at most 128 MiB of HBM per device.

v0:
```python
import jax
import jax.numpy as jnp
from jax import lax
from jax.sharding import PartitionSpec as P

HEADS = 16
DH = 128
MBLK = 128
EXPIRED = 4
MASKED = -1e30


def fold_piece(softmax_state, query_rows, key_rows, value_rows, key_mask):
    old_max, old_sum, old_acc = softmax_state
    scores = jnp.einsum(
        "thd,shd->hts", query_rows, key_rows, preferred_element_type=jnp.float32
    ) * query_rows.shape[2] ** (-0.5)
    scores = jnp.where(key_mask[None], scores, MASKED)
    row_max = jnp.maximum(old_max, jnp.max(scores, -1))
    exp_scores = jnp.where(key_mask[None], jnp.exp(scores - row_max[:, :, None]), 0.0)
    new_sum = jnp.sum(exp_scores, -1)
    new_acc = jnp.einsum(
        "hts,shd->htd",
        exp_scores.astype(jnp.bfloat16),
        value_rows,
        preferred_element_type=jnp.float32,
    )
    return (row_max, new_sum, new_acc)


def on_device(
    queries,
    seq_keys,
    seq_values,
    memory_keys,
    memory_values,
    retrieval,
    fifo_head,
    head_gate,
    norm_gain,
):
    tok_rows, head_count, head_width = queries.shape
    seq_devices = lax.axis_size("seq")
    my_index = lax.axis_index("seq")
    block_count = seq_devices * tok_rows // MBLK
    query_pos = my_index * tok_rows + jnp.arange(tok_rows, dtype=jnp.int32)
    wanted = retrieval[0]
    head_pos = fifo_head[0]

    def fresh_state():
        return (
            jnp.full((head_count, tok_rows), MASKED, jnp.float32),
            jnp.zeros((head_count, tok_rows), jnp.float32),
            jnp.zeros((head_count, tok_rows, head_width), jnp.float32),
        )

    pieces = (
        lax.all_gather(seq_keys, "seq", axis=0, tiled=True),
        lax.all_gather(seq_values, "seq", axis=0, tiled=True),
    )
    key_pos = jnp.arange(pieces[0].shape[0], dtype=jnp.int32)
    local_state = fold_piece(
        fresh_state(), queries, pieces[0], pieces[1], key_pos[None, :] <= query_pos[:, None]
    )
    pieces = (
        lax.all_gather(memory_keys, "seq", axis=0, tiled=True),
        lax.all_gather(memory_values, "seq", axis=0, tiled=True),
    )
    row_count = pieces[0].shape[0]
    block_ids = jnp.arange(row_count, dtype=jnp.int32) // MBLK
    is_live = jnp.mod(block_ids - head_pos + block_count, block_count) >= EXPIRED
    block_ids, is_live = (block_ids, is_live)
    chosen = jnp.any(block_ids[:, None] == wanted[None, :], -1) & is_live
    memory_state = fold_piece(
        fresh_state(),
        queries,
        pieces[0],
        pieces[1],
        jnp.broadcast_to(chosen[None, :], (tok_rows, row_count)),
    )
    local_out = local_state[2] / local_state[1][:, :, None]
    memory_out = memory_state[2] / memory_state[1][:, :, None]
    gate_mix = jax.nn.sigmoid(head_gate)[:, None, None]
    combined = gate_mix * memory_out + (1.0 - gate_mix) * local_out
    squares = lax.psum(jnp.sum(combined * combined, axis=(0, 2)), "head")
    row_scale = lax.rsqrt(squares / (HEADS * DH) + 1e-06)
    result = combined * row_scale[None, :, None] * norm_gain[:, None, :]
    return jnp.transpose(result, (1, 0, 2)).astype(jnp.bfloat16)


def solution(mesh):
    in_specs = (
        P("seq", "head", None),
        P("seq", "head", None),
        P("seq", "head", None),
        P("seq", "head", None),
        P("seq", "head", None),
        P("seq", None),
        P(),
        P("head"),
        P("head", None),
    )
    out_specs = P("seq", "head", None)
    return jax.shard_map(
        on_device, mesh=mesh, in_specs=in_specs, out_specs=out_specs, check_vma=False
    )
```

profile of v0, /device:TPU:1, one launch (start us, length us, event | category | flops | bytes accessed | tf_op | source)
XLA Modules:
  0.0 618.5 jit_solution(12764481445013468850)
XLA Ops:
  6.5 1.5 copy.17
  8.1 0.0 all-gather.9.cloned.1.call-start
  8.1 1.5 copy.20
  9.6 0.0 all-gather.7.cloned.1.call-start
  9.7 1.6 copy.19
  11.3 1.6 copy.22
  13.6 0.8 compare_reduce_fusion
  14.4 0.7 broadcast_subtract_fusion
  15.1 0.7 iota_compare_fusion
  15.8 138.3 %all-gather.5.cloned.1.call-done = bf16[8192,2,128]{2,0,1:T(8,128)(2,1)} async-done(((bf16[128,2,128]{2,0,1:T(8,128)(2,1)}), bf16[8192,2,128]{2,0,1:T(8,128)(2,1)}) %all-gather.5.cloned.1.call-update) | async-done | bytes 4194320 | tf_op jit(solution)/shard_map/all_gather | solution.py:66
  154.1 6.8 %fusion.33 = (f32[2,128]{1,0:T(2,128)S(1)}, f32[2,128,8192]{2,1,0:T(8,128)}) fusion(bf16[8192,2,128]{2,0,1:T(8,128)(2,1)} %all-gather.5.cloned.1.call-done, bf16[128,2,128]{2,1,0:T(2,128)(2,1)} %param.9, pred[8192]{0:T(1024)(128)(4,1)S(1)} %fusion.29), kind=kOutput, calls=%fused_computation.53 | convolution fusion | flops 543162112 | bytes 12657664 | tf_op jit(solution)/shard_map/thd,shd->hts/dot_general | solution.py:15
  160.9 137.4 %all-gather.9.cloned.1.call-done = bf16[8192,2,128]{2,0,1:T(8,128)(2,1)} async-done(((bf16[128,2,128]{2,0,1:T(8,128)(2,1)}), bf16[8192,2,128]{2,0,1:T(8,128)(2,1)}) %all-gather.9.cloned.1.call-update) | async-done | bytes 4194320 | tf_op jit(solution)/shard_map/all_gather | solution.py:58
  298.3 4.5 fusion.32
  302.8 0.1 copy-done.1
  303.0 1.8 fusion.2
  304.8 1.3 copy-done
  306.0 2.1 fusion.4
  308.2 132.3 %all-gather.7.cloned.1.call-done = bf16[8192,2,128]{0,2,1:T(8,128)(2,1)} async-done(((bf16[128,2,128]{0,2,1:T(8,128)(2,1)}), bf16[8192,2,128]{0,2,1:T(8,128)(2,1)}) %all-gather.7.cloned.1.call-update) | async-done | bytes 4194320 | tf_op jit(solution)/shard_map/all_gather | solution.py:67
  440.5 6.0 fusion.8
  446.5 136.7 %all-gather.11.cloned.1.call-done = bf16[8192,2,128]{0,2,1:T(8,128)(2,1)} async-done(((bf16[128,2,128]{0,2,1:T(8,128)(2,1)}), bf16[8192,2,128]{0,2,1:T(8,128)(2,1)}) %all-gather.11.cloned.1.call-update) | async-done | bytes 4194320 | tf_op jit(solution)/shard_map/all_gather | solution.py:59
  583.2 6.3 %multiply_reduce_fusion = (f32[128]{0:T(128)S(1)}, f32[2,128,128]{1,2,0:T(8,128)S(1)}) fusion(f32[2,128,128]{1,2,0:T(8,128)S(1)} %fusion.8, f32[2,128]{1,0:T(2,128)S(1)} %fusion.4, f32[2]{0:T(128)S(1)} %get-tuple-element.5, f32[2,128]{1,0:T(2,128)S(1)} %fusion.2, f32[2]{0:T(128)S(1)} %get-tuple-element.6, ...), kind=kOutput, calls=%fused_computation.27 | convolution fusion | flops 543391616 | bytes 13897232 | tf_op jit(solution)/shard_map/hts,shd->htd/dot_general | solution.py:22
  589.5 21.6 %psum.7 = f32[128]{0:T(128)S(1)} all-reduce(f32[128]{0:T(128)S(1)} %get-tuple-element.11), channel_id=1, replica_groups=mesh['seq'=64,'head'=8] {'head'}, use_global_device_ids=true, to_apply=%region_6.7 | all-reduce | flops 128 | bytes 1024 | tf_op jit(solution)/shard_map/psum | solution.py:85
  611.1 0.1 fusion.21
  611.2 0.8 copy.23
  (18 shorter events, 0.2 us)
Async XLA Ops:
  6.5 291.8 %copy-start.2 = (bf16[128,2,128]{2,1,0:T(2,128)(2,1)S(1)}, bf16[128,2,128]{2,1,0:T(2,128)(2,1)}, u32[]{:S(2)}) copy-start(bf16[128,2,128]{2,1,0:T(2,128)(2,1)} %param.9) | copy-start | bytes 196612
  6.5 147.6 %all-gather.5.cloned.1.call-start = ((), (), s32[]{:S(2)}) async-start(), calls=%async_computation | async-start | bytes 4259840 | tf_op jit(solution)/shard_map/all_gather | solution.py:66
  8.1 290.3 %all-gather.9.cloned.1.call-start = ((), (), s32[]{:S(2)}) async-start(), calls=%async_computation.2 | async-start | bytes 4259840 | tf_op jit(solution)/shard_map/all_gather | solution.py:58
  9.6 430.9 %all-gather.7.cloned.1.call-start = ((), (), s32[]{:S(2)}) async-start(), calls=%async_computation.1 | async-start | bytes 4259840 | tf_op jit(solution)/shard_map/all_gather | solution.py:67
  11.3 571.9 %all-gather.11.cloned.1.call-start = ((), (), s32[]{:S(2)}) async-start(), calls=%async_computation.3 | async-start | bytes 4259840 | tf_op jit(solution)/shard_map/all_gather | solution.py:59
  298.3 4.6 copy-start.1
  302.8 3.2 copy-start
  583.2 28.0 %copy-start.3 = (f32[2,128]{1,0:T(2,128)S(1)}, f32[2,128]{1,0:T(2,128)}, u32[]{:S(2)}) copy-start(f32[2,128]{1,0:T(2,128)} %param.17) | copy-start | bytes 3076
Sparse Core Ops, SparseCore 0:
  10.3 143.7 all-gather.4
  157.1 141.2 all-gather.8
  301.2 139.1 all-gather.6
  443.2 139.8 all-gather.10
where the time goes:
time: 619 us
  waiting for transfers between devices  545 us (88%)
  matrix products  23.6 us (4%)
  blocking collectives  21.6 us (3%)
  between operations  13.8 us (2%)
  local copies, waits for them, and re-layouts  8.29 us (1%)
  other arithmetic  6.25 us (1%)
    all_gather x1, waiting for transfers between devices, on_device(): lax.all_gather(memory_keys, 'seq', axis=0, tiled=True)  138 us
    all_gather x1, waiting for transfers between devices, on_device(): lax.all_gather(seq_keys, 'seq', axis=0, tiled=True)  137 us
    all_gather x1, waiting for transfers between devices, on_device(): lax.all_gather(seq_values, 'seq', axis=0, tiled=True)  137 us
    all_gather x1, waiting for transfers between devices, on_device(): lax.all_gather(memory_values, 'seq', axis=0, tiled=True)  132 us
    psum x1, blocking collectives, on_device(): squares = lax.psum(jnp.sum(combined * combined, axis=(0, 2)), 'head')  21.6 us
  transfers between devices with their start and end apart: 4, of which 4 were waited for; matrix products, arithmetic and copies ran while one was open for 5% of the time, Pallas kernels for 0%

commit v1 on v0

--- a/solution.py
+++ b/solution.py
@@ -54,10 +54,12 @@
             jnp.zeros((head_count, tok_rows, head_width), jnp.float32),
         )
 
-    pieces = (
-        lax.all_gather(seq_keys, "seq", axis=0, tiled=True),
-        lax.all_gather(seq_values, "seq", axis=0, tiled=True),
-    )
+    def recast_units(page):
+        small = jnp.stack([page for _ in range(lax.axis_size("seq"))], 0)
+        new = lax.all_to_all(small, "seq", 0, 0)
+        return jnp.concatenate(new, 0)
+
+    pieces = (recast_units(seq_keys), lax.all_gather(seq_values, "seq", axis=0, tiled=True))
     key_pos = jnp.arange(pieces[0].shape[0], dtype=jnp.int32)
     local_state = fold_piece(
         fresh_state(), queries, pieces[0], pieces[1], key_pos[None, :] <= query_pos[:, None]

time: 619 us -> 563 us (0.910)
  waiting for transfers between devices: 545 us -> 468 us
  starting transfers between devices: 0.13 us -> 19.5 us
  local copies, waits for them, and re-layouts: 8.29 us -> 16.8 us
    all_gather x1 -> x0, waiting for transfers between devices: 137 us -> none  [on_device(): lax.all_gather(seq_keys, 'seq', axis=0, tiled=True)]
    all_gather x1, waiting for transfers between devices: 138 us -> 210 us  [on_device(): lax.all_gather(memory_keys, 'seq', axis=0, tiled=True)]
    all_to_all x0 -> x1, starting transfers between devices: none -> 19.4 us  [recast_units(): new = lax.all_to_all(small, 'seq', 0, 0)]
    all_gather x1, waiting for transfers between devices: 137 us -> 127 us  [on_device(): lax.all_gather(seq_values, 'seq', axis=0, tiled=True)]
  transfers between devices with their start and end apart: 4 -> 4, of which waited for: 4 -> 3; matrix products, arithmetic and copies ran while one was open for 5% -> 4% of each run, Pallas kernels for 0% -> 0%
where the time goes in v1:
time: 563 us
  waiting for transfers between devices  468 us (83%)
  blocking collectives  21.6 us (4%)
  starting transfers between devices  19.5 us (3%)
  matrix products  18.1 us (3%)
  local copies, waits for them, and re-layouts  16.8 us (3%)
  between operations  13.9 us (2%)
    all_gather x1, waiting for transfers between devices, on_device(): lax.all_gather(memory_keys, 'seq', axis=0, tiled=True)  210 us
    all_gather x1, waiting for transfers between devices, on_device(): lax.all_gather(memory_values, 'seq', axis=0, tiled=True)  132 us
    all_gather x1, waiting for transfers between devices, on_device(): lax.all_gather(seq_values, 'seq', axis=0, tiled=True)  127 us
    psum x1, blocking collectives, on_device(): squares = lax.psum(jnp.sum(combined * combined, axis=(0, 2)), 'head')  21.6 us
    all_to_all x1, starting transfers between devices, recast_units(): new = lax.all_to_all(small, 'seq', 0, 0)  19.4 us
    dot_general x2, matrix products, fold_piece(): jnp.einsum('hts,shd->htd', exp_scores.astype(jnp.bfloat16), value_rows, p...  12.3 us
  transfers between devices with their start and end apart: 4, of which 3 were waited for; matrix products, arithmetic and copies ran while one was open for 4% of the time, Pallas kernels for 0%

profile of v1, /device:TPU:1, one launch (start us, length us, event | category | flops | bytes accessed | tf_op | source)
XLA Modules:
  0.0 562.9 jit_solution(11009289937705777814)
XLA Ops:
  6.6 1.5 copy.25
  8.1 0.9 copy.28
  9.0 3.0 stack.2
  12.0 19.4 %all-to-all-start = ((bf16[64,128,2,128]{3,1,2,0:T(8,128)(2,1)}), bf16[64,128,2,128]{3,1,2,0:T(8,128)(2,1)}, u32[]{:S(2)}, u32[]{:S(2)}) async-start(bf16[64,128,2,128]{3,1,2,0:T(8,128)(2,1)} %stack.2), calls=%async_computation | async-start | bytes 8388608 | tf_op jit(solution)/shard_map/all_to_all | solution.py:59
  31.4 0.0 all-gather.6.cloned.1.call-start
  31.4 0.7 copy.27
  32.3 0.8 copy.31
  33.7 0.2 compare_reduce_fusion
  33.9 0.7 iota_compare_fusion
  34.6 209.6 %all-gather.4.cloned.1.call-done = bf16[8192,2,128]{2,0,1:T(8,128)(2,1)} async-done(((bf16[128,2,128]{2,0,1:T(8,128)(2,1)}), bf16[8192,2,128]{2,0,1:T(8,128)(2,1)}) %all-gather.4.cloned.1.call-update) | async-done | bytes 4194320 | tf_op jit(solution)/shard_map/all_gather | solution.py:68
  244.2 3.6 fusion.33
  247.9 3.2 copy-done.1
  251.1 1.8 fusion.2
  252.9 131.8 %all-gather.6.cloned.1.call-done = bf16[8192,2,128]{0,2,1:T(8,128)(2,1)} async-done(((bf16[128,2,128]{0,2,1:T(8,128)(2,1)}), bf16[8192,2,128]{0,2,1:T(8,128)(2,1)}) %all-gather.6.cloned.1.call-update) | async-done | bytes 4194320 | tf_op jit(solution)/shard_map/all_gather | solution.py:69
  384.7 6.0 %fusion.8 = f32[2,128,128]{1,2,0:T(8,128)S(1)} fusion(bf16[8192,2,128]{0,2,1:T(8,128)(2,1)} %all-gather.6.cloned.1.call-done, f32[2,128,8192]{2,1,0:T(8,128)} %copy-done.1, f32[2,128]{1,0:T(2,128)S(1)} %broadcast_maximum_fusion.1, pred[8192]{0:T(1024)(128)(4,1)S(1)} %fusion.29), kind=kOutput, calls=%fused_computation.11 | convolution fusion | flops 543162368 | bytes 12723200 | tf_op jit(solution)/shard_map/hts,shd->htd/dot_general | solution.py:22
  390.7 2.7 copy.29
  393.4 2.2 fusion.32
  395.7 3.2 copy-done
  398.9 2.1 fusion.4
  401.0 126.5 %all-gather.8.cloned.1.call-done = bf16[8192,2,128]{0,2,1:T(8,128)(2,1)} async-done(((bf16[128,2,128]{0,2,1:T(8,128)(2,1)}), bf16[8192,2,128]{0,2,1:T(8,128)(2,1)}) %all-gather.8.cloned.1.call-update) | async-done | bytes 4194320 | tf_op jit(solution)/shard_map/all_gather | solution.py:62
  527.5 6.3 %multiply_reduce_fusion = (f32[128]{0:T(128)S(1)}, f32[2,128,128]{1,2,0:T(8,128)S(1)}) fusion(f32[2,128,128]{1,2,0:T(8,128)S(1)} %fusion.8, f32[2,128]{1,0:T(2,128)S(1)} %fusion.4, f32[2]{0:T(128)S(1)} %get-tuple-element.5, f32[2,128]{1,0:T(2,128)S(1)} %fusion.2, f32[2]{0:T(128)S(1)} %get-tuple-element.6, ...), kind=kOutput, calls=%fused_computation.27 | convolution fusion | flops 543391616 | bytes 13897232 | tf_op jit(solution)/shard_map/hts,shd->htd/dot_general | solution.py:22
  533.8 21.6 %psum.7 = f32[128]{0:T(128)S(1)} all-reduce(f32[128]{0:T(128)S(1)} %get-tuple-element.11), channel_id=1, replica_groups=mesh['seq'=64,'head'=8] {'head'}, use_global_device_ids=true, to_apply=%region_6.7 | all-reduce | flops 128 | bytes 1024 | tf_op jit(solution)/shard_map/psum | solution.py:87
  555.5 0.1 fusion.21
  555.6 0.8 copy.32
  (27 shorter events, 0.2 us)
Async XLA Ops:
  6.5 24.9 %copy-start.3 = (bf16[128,2,128]{2,1,0:T(2,128)(2,1)S(1)}, bf16[128,2,128]{2,1,0:T(2,128)(2,1)}, u32[]{:S(2)}) copy-start(bf16[128,2,128]{2,1,0:T(2,128)(2,1)} %param.13) | copy-start | bytes 196612
  6.5 25.7 %copy-start.4 = (bf16[128,2,128]{2,1,0:T(2,128)(2,1)S(1)}, bf16[128,2,128]{2,1,0:T(2,128)(2,1)}, u32[]{:S(2)}) copy-start(bf16[128,2,128]{2,1,0:T(2,128)(2,1)} %param.11) | copy-start | bytes 196612
  6.5 27.2 %copy-start.6 = (s32[1,8]{1,0:T(1,128)S(1)}, s32[1,8]{1,0:T(1,128)}, u32[]{:S(2)}) copy-start(s32[1,8]{1,0:T(1,128)} %param.14) | copy-start | bytes 100
  6.5 27.3 %copy-start.7 = (f32[2]{0:T(128)S(1)}, f32[2]{0:T(128)}, u32[]{:S(2)}) copy-start(f32[2]{0:T(128)} %param.16) | copy-start | bytes 28
  6.5 237.7 %copy-start.2 = (bf16[128,2,128]{2,1,0:T(2,128)(2,1)S(1)}, bf16[128,2,128]{2,1,0:T(2,128)(2,1)}, u32[]{:S(2)}) copy-start(bf16[128,2,128]{2,1,0:T(2,128)(2,1)} %param.9) | copy-start | bytes 196612
  6.5 237.7 %all-gather.4.cloned.1.call-start = ((), (), s32[]{:S(2)}) async-start(), calls=%async_computation.1 | async-start | bytes 4259840 | tf_op jit(solution)/shard_map/all_gather | solution.py:68
  12.0 378.7 %all-to-all-start = ((bf16[64,128,2,128]{3,1,2,0:T(8,128)(2,1)}), bf16[64,128,2,128]{3,1,2,0:T(8,128)(2,1)}, u32[]{:S(2)}, u32[]{:S(2)}) async-start(bf16[64,128,2,128]{3,1,2,0:T(8,128)(2,1)} %stack.2), calls=%async_computation | async-start | bytes 8388608 | tf_op jit(solution)/shard_map/all_to_all | solution.py:59
  31.4 353.3 %all-gather.6.cloned.1.call-start = ((), (), s32[]{:S(2)}) async-start(), calls=%async_computation.2 | async-start | bytes 4259840 | tf_op jit(solution)/shard_map/all_gather | solution.py:69
  32.2 495.3 %all-gather.8.cloned.1.call-start = ((), (), s32[]{:S(2)}) async-start(), calls=%async_computation.3 | async-start | bytes 4259840 | tf_op jit(solution)/shard_map/all_gather | solution.py:62
  247.8 3.2 copy-start.1
  395.7 3.2 copy-start
  527.5 28.0 %copy-start.5 = (f32[2,128]{1,0:T(2,128)S(1)}, f32[2,128]{1,0:T(2,128)}, u32[]{:S(2)}) copy-start(f32[2,128]{1,0:T(2,128)} %param.17) | copy-start | bytes 3076
Sparse Core Ops, SparseCore 0:
  10.3 233.8 all-gather.3
  247.1 137.5 all-gather.5
  387.6 139.8 all-gather.7
